TPU v7x, 512 devices: a whole 4x4x16 slice. The times are simulated.
512 devices in a mesh: tm: 64 (over x, z), row: 8 (over y, core).
Axes of the slice: x: 4, y: 4, z: 16, core: 2. Of those that a mesh axis runs over, the one named last changes fastest.
Arguments:
- observations: bfloat16 [256, 128], P('tm'), may hold values from -6 to 6
- gain: bfloat16 [1024, 128], replicated, may hold values from -1 to 1
- damping: float32 [256, 1024], P('tm'), may hold values from 0.4 to 1
- blocks: bfloat16 [256, 1024, 128], P('tm', 'row'), may hold values from -0.109375 to 0.109375
- pattern: int32 [64, 8], replicated, may hold values from 0 to 63, as said below
- sensor_index: int32 [128], replicated, may hold values from 0 to 1023, as said below
Outputs:
- element_matrix: bfloat16 [64, 1024, 1024], P('tm', 'row')
- element_vector: float32 [64, 1024], P('tm', 'row')
Inputs may be any that keep to these rules, and one draw needn't show every extreme that they name: `pattern`: each block row names 8 different block columns. `sensor_index`: the sensors observe different states.
All inputs are finite; a program needn't handle non-finite values.
Results may differ from a plain program's by a relative error of at most 0.035.
Values may be sent and summed in bfloat16 or wider, within the bound.
A program may use at most 64 MiB of HBM per device.

v0:
```python
import jax
import jax.numpy as jnp
from jax import lax
from jax.sharding import PartitionSpec as P

STATES = 1024
BS = 16
S = 8
STRETCH = 4
LEVELS = 4
NBLK = 64


def shifted(block, axis, distance):
    devices = range(lax.axis_size(axis))
    route = [(i - distance, i) for i in devices if i - distance in devices]
    return lax.ppermute(block, axis, route)


def sparse_rows(weighted, piece, pattern):
    block_count = piece.shape[0] // BS
    row_count = weighted.shape[0]
    selector = (pattern[:, :, None] == jnp.arange(NBLK, dtype=jnp.int32)[None, None, :]).astype(
        jnp.float32
    )
    columns = weighted.reshape(row_count, block_count, BS)
    grouped = piece.reshape(block_count, BS, S, BS)
    partial_value = jnp.einsum(
        "irk,rksl->rsli", columns, grouped, preferred_element_type=jnp.float32
    )
    placed = jnp.einsum("rsc,rsli->cli", selector, partial_value, precision=lax.Precision.HIGHEST)
    return placed.reshape(STATES, row_count).T


def shards(observations, gain, damping, blocks, pattern, sensor_index):
    row_count = blocks.shape[1]
    first_row = lax.axis_index("row") * row_count
    carry = (
        jnp.arange(STATES, dtype=jnp.int32)[None, :]
        == (first_row + jnp.arange(row_count, dtype=jnp.int32))[:, None]
    ).astype(jnp.float32)
    offset = jnp.zeros((row_count,), jnp.float32)
    innovation = jnp.dot(observations, gain.T, preferred_element_type=jnp.float32)
    gain_wide = gain.astype(jnp.float32)
    for step in reversed(range(STRETCH)):
        offset = offset + jnp.dot(carry, innovation[step], precision=lax.Precision.HIGHEST)
        through_gain = jnp.dot(carry, gain_wide, precision=lax.Precision.HIGHEST)
        weighted = carry.at[:, sensor_index].add(-through_gain).astype(jnp.bfloat16)
        product = sparse_rows(
            weighted, lax.all_gather(blocks[step], "row", axis=0, tiled=True), pattern
        )
        carry = weighted.astype(jnp.float32) * damping[step][None, :] + product
    matrix = carry.astype(jnp.bfloat16)
    vector = offset
    time_index = lax.axis_index("tm")
    for level in range(LEVELS):
        span = 2**level
        full_matrix, full_vector = (
            lax.all_gather(matrix, "row", axis=0, tiled=True),
            lax.all_gather(vector.astype(jnp.bfloat16), "row", axis=0, tiled=True).astype(
                vector.dtype
            ),
        )
        earlier_matrix, earlier_vector = (
            shifted(full_matrix, "tm", span),
            shifted(full_vector.astype(jnp.bfloat16), "tm", span).astype(full_vector.dtype),
        )
        joined_matrix = jnp.dot(matrix, earlier_matrix, preferred_element_type=jnp.float32)
        joined_vector = jnp.dot(
            matrix.astype(jnp.float32), earlier_vector, precision=lax.Precision.HIGHEST
        )
        active = time_index % (2 * span) == 2 * span - 1
        new_vector = joined_vector + vector
        matrix = jnp.where(active, joined_matrix.astype(jnp.bfloat16), matrix)
        vector = jnp.where(active, new_vector, vector)
    return (matrix[None, :, :], vector[None, :])


def solution(mesh):
    return jax.shard_map(
        shards,
        mesh=mesh,
        in_specs=(P("tm", None), P(), P("tm", None), P("tm", "row", None), P(), P()),
        out_specs=(P("tm", "row", None), P("tm", "row")),
        check_vma=False,
    )
```

profile of v0, /device:TPU:36, one launch (start us, length us, event | category | flops | bytes accessed | tf_op | source)
XLA Modules:
  0.0 864.4 jit_solution(12641825661058626743)
XLA Ops:
  7.3 0.8 copy-done
  8.1 0.3 fusion.28
  8.5 0.7 compare_select_fusion
  9.2 1.4 scatter_fusion
  10.7 13.4 %all-gather = bf16[1,1024,128]{2,1,0:T(8,128)(2,1)S(1)} all-gather(bf16[1,128,128]{2,1,0:T(8,128)(2,1)S(1)} %get-tuple-element.2), channel_id=2, replica_groups=mesh['tm'=64,'row'=8] {'row'}, dimensions={1}, use_global_device_ids=true | all-gather | bytes 294912 | tf_op jit(solution)/shard_map/all_gather | solution.py:50
  24.1 2.4 reshape.46
  26.5 3.4 copy.25
  29.9 0.7 fusion.57
  30.6 4.2 fusion.8
  34.8 0.3 copy.27
  35.8 0.6 fusion.27
  36.4 0.4 fusion.40
  36.9 1.5 scatter_fusion.1
  38.4 13.3 %all-gather.1 = bf16[1,1024,128]{2,1,0:T(8,128)(2,1)S(1)} all-gather(bf16[1,128,128]{2,1,0:T(8,128)(2,1)S(1)} %get-tuple-element.3), channel_id=3, replica_groups=mesh['tm'=64,'row'=8] {'row'}, dimensions={1}, use_global_device_ids=true | all-gather | bytes 294912 | tf_op jit(solution)/shard_map/all_gather | solution.py:50
  51.7 2.4 reshape.49
  54.1 3.4 copy.29
  57.5 0.7 fusion.58
  58.1 4.2 fusion.11
  62.3 0.3 copy.31
  62.8 0.4 fusion.39
  63.2 0.6 fusion.26
  63.9 1.5 scatter_fusion.2
  65.4 13.0 %all-gather.2 = bf16[1,1024,128]{2,1,0:T(8,128)(2,1)S(1)} all-gather(bf16[1,128,128]{2,1,0:T(8,128)(2,1)S(1)} %get-tuple-element.5), channel_id=4, replica_groups=mesh['tm'=64,'row'=8] {'row'}, dimensions={1}, use_global_device_ids=true | all-gather | bytes 294912 | tf_op jit(solution)/shard_map/all_gather | solution.py:50
  78.4 2.4 reshape.52
  80.8 3.4 copy.33
  84.2 0.7 fusion.59
  84.9 4.2 fusion.14
  89.6 0.6 fusion.25
  90.2 0.4 fusion.38
  90.7 1.5 scatter_fusion.3
  92.5 13.1 %all-gather.3 = bf16[1,1024,128]{2,1,0:T(8,128)(2,1)S(1)} all-gather(bf16[1,128,128]{2,1,0:T(8,128)(2,1)S(1)} %get-tuple-element.4), channel_id=5, replica_groups=mesh['tm'=64,'row'=8] {'row'}, dimensions={1}, use_global_device_ids=true | all-gather | bytes 294912 | tf_op jit(solution)/shard_map/all_gather | solution.py:50
  105.5 2.4 reshape.55
  107.9 3.4 copy.39
  111.3 0.7 fusion.60
  112.0 4.2 fusion.17
  116.6 0.8 fusion.41
  117.5 36.3 %all-gather.13.cloned.1.call-done = bf16[1024,1024]{1,0:T(8,128)(2,1)} async-done(((bf16[128,1024]{1,0:T(8,128)(2,1)}), bf16[1024,1024]{1,0:T(8,128)(2,1)}) %all-gather.13.cloned.1.call-update) | async-done | bytes 2097168 | tf_op jit(solution)/shard_map/all_gather | solution.py:59
  153.8 3.5 collective-permute-start
  157.3 46.4 %collective-permute-done = bf16[1024,1024]{1,0:T(8,128)(2,1)S(1)} collective-permute-done((bf16[1024,1024]{1,0:T(8,128)(2,1)}, bf16[1024,1024]{1,0:T(8,128)(2,1)S(1)}, u32[]{:S(2)}, u32[]{:S(2)}) %collective-permute-start) | collective-permute-done | bytes 2097184 | tf_op jit(solution)/shard_map/ppermute | solution.py:17
  203.7 2.2 fusion.23
  206.0 34.5 %all-gather.15.cloned.1.call-done = bf16[1024,1024]{1,0:T(8,128)(2,1)} async-done(((bf16[128,1024]{1,0:T(8,128)(2,1)}), bf16[1024,1024]{1,0:T(8,128)(2,1)}) %all-gather.15.cloned.1.call-update) | async-done | bytes 2097168 | tf_op jit(solution)/shard_map/all_gather | solution.py:59
  240.5 4.4 collective-permute-start.1
  245.0 93.4 %collective-permute-done.1 = bf16[1024,1024]{1,0:T(8,128)(2,1)S(1)} collective-permute-done((bf16[1024,1024]{1,0:T(8,128)(2,1)}, bf16[1024,1024]{1,0:T(8,128)(2,1)S(1)}, u32[]{:S(2)}, u32[]{:S(2)}) %collective-permute-start.1) | collective-permute-done | bytes 2097184 | tf_op jit(solution)/shard_map/ppermute | solution.py:17
  338.3 2.2 fusion.22
  340.6 32.6 %all-gather.17.cloned.1.call-done = bf16[1024,1024]{1,0:T(8,128)(2,1)} async-done(((bf16[128,1024]{1,0:T(8,128)(2,1)}), bf16[1024,1024]{1,0:T(8,128)(2,1)}) %all-gather.17.cloned.1.call-update) | async-done | bytes 2097168 | tf_op jit(solution)/shard_map/all_gather | solution.py:59
  373.2 7.6 collective-permute-start.2
  380.8 182.3 %collective-permute-done.2 = bf16[1024,1024]{1,0:T(8,128)(2,1)S(1)} collective-permute-done((bf16[1024,1024]{1,0:T(8,128)(2,1)}, bf16[1024,1024]{1,0:T(8,128)(2,1)S(1)}, u32[]{:S(2)}, u32[]{:S(2)}) %collective-permute-start.2) | collective-permute-done | bytes 2097184 | tf_op jit(solution)/shard_map/ppermute | solution.py:17
  563.1 2.2 fusion.21
  565.4 31.8 %all-gather.19.cloned.1.call-done = bf16[1024,1024]{1,0:T(8,128)(2,1)} async-done(((bf16[128,1024]{1,0:T(8,128)(2,1)}), bf16[1024,1024]{1,0:T(8,128)(2,1)}) %all-gather.19.cloned.1.call-update) | async-done | bytes 2097168 | tf_op jit(solution)/shard_map/all_gather | solution.py:59
  597.1 11.9 %collective-permute-start.3 = (bf16[1024,1024]{1,0:T(8,128)(2,1)}, bf16[1024,1024]{1,0:T(8,128)(2,1)S(1)}, u32[]{:S(2)}, u32[]{:S(2)}) collective-permute-start(bf16[1024,1024]{1,0:T(8,128)(2,1)} %all-gather.19.cloned.1.call-done), channel_id=1, source_target_pairs={{0,64},{8,72},{16,80},{24,88},{32,96},{40,104},{48,112},{56,120},{... | collective-permute-start | bytes 6291464 | tf_op jit(solution)/shard_map/ppermute | solution.py:17
  609.0 9.5 %all-gather.4 = bf16[8,1,128]{2,1,0:T(2,128)(2,1)S(1)} all-gather(bf16[1,1,128]{2,1,0:T(2,128)(2,1)S(1)} %convert_bitcast_fusion.3), channel_id=1, replica_groups=mesh['tm'=64,'row'=8] {'row'}, dimensions={0}, use_global_device_ids=true | all-gather | bytes 2304 | tf_op jit(solution)/shard_map/all_gather | solution.py:60
  618.5 2.6 collective-permute-start.4
  621.1 170.8 %collective-permute-done.4 = bf16[1024]{0:T(1024)(128)(2,1)S(1)} collective-permute-done((bf16[1024]{0:T(1024)(128)(2,1)S(1)}, bf16[1024]{0:T(1024)(128)(2,1)S(1)}, u32[]{:S(2)}, u32[]{:S(2)}) %collective-permute-start.4) | collective-permute-done | bytes 2080 | tf_op jit(solution)/shard_map/ppermute | solution.py:17
  792.1 9.9 %all-gather.5 = bf16[8,1,128]{2,1,0:T(2,128)(2,1)S(1)} all-gather(bf16[1,1,128]{2,1,0:T(2,128)(2,1)S(1)} %convert_bitcast_fusion.2), channel_id=1, replica_groups=mesh['tm'=64,'row'=8] {'row'}, dimensions={0}, use_global_device_ids=true | all-gather | bytes 2304 | tf_op jit(solution)/shard_map/all_gather | solution.py:60
  802.0 1.9 collective-permute-start.5
  803.9 6.6 collective-permute-done.5
  810.7 7.8 all-gather.6
  818.5 1.9 collective-permute-start.6
  820.4 8.4 collective-permute-done.6
  829.0 9.7 %all-gather.7 = bf16[8,1,128]{2,1,0:T(2,128)(2,1)S(1)} all-gather(bf16[1,1,128]{2,1,0:T(2,128)(2,1)S(1)} %convert_bitcast_fusion), channel_id=1, replica_groups=mesh['tm'=64,'row'=8] {'row'}, dimensions={0}, use_global_device_ids=true | all-gather | bytes 2304 | tf_op jit(solution)/shard_map/all_gather | solution.py:60
  838.7 1.9 collective-permute-start.7
  840.7 13.2 %collective-permute-done.7 = bf16[1024]{0:T(1024)(128)(2,1)S(1)} collective-permute-done((bf16[1024]{0:T(1024)(128)(2,1)S(1)}, bf16[1024]{0:T(1024)(128)(2,1)S(1)}, u32[]{:S(2)}, u32[]{:S(2)}) %collective-permute-start.7) | collective-permute-done | bytes 2080 | tf_op jit(solution)/shard_map/ppermute | solution.py:17
  853.8 1.6 fusion.31
  855.5 2.2 fusion.24
  (60 shorter events, 3.7 us)
Async XLA Ops:
  7.2 1.0 copy-start
  7.2 3.5 copy-start.4
  7.2 146.7 %all-gather.13.cloned.1.call-start = ((), (), s32[]{:S(2)}) async-start(), calls=%async_computation | async-start | bytes 2359296 | tf_op jit(solution)/shard_map/all_gather | solution.py:59
  29.9 0.7 copy-start.5
  30.6 4.5 copy-start.6
  30.6 4.5 copy-start.7
  117.5 123.0 %all-gather.15.cloned.1.call-start = ((), (), s32[]{:S(2)}) async-start(), calls=%async_computation.1 | async-start | bytes 2359296 | tf_op jit(solution)/shard_map/all_gather | solution.py:59
  153.8 49.9 %collective-permute-start = (bf16[1024,1024]{1,0:T(8,128)(2,1)}, bf16[1024,1024]{1,0:T(8,128)(2,1)S(1)}, u32[]{:S(2)}, u32[]{:S(2)}) collective-permute-start(bf16[1024,1024]{1,0:T(8,128)(2,1)} %all-gather.13.cloned.1.call-done), channel_id=1, source_target_pairs={{0,8},{8,16},{16,24},{24,32},{32,40},{40,48},{48,56},{56,64},{64,7... | collective-permute-start | bytes 6291464 | tf_op jit(solution)/shard_map/ppermute | solution.py:17
  205.9 167.2 %all-gather.17.cloned.1.call-start = ((), (), s32[]{:S(2)}) async-start(), calls=%async_computation.2 | async-start | bytes 2359296 | tf_op jit(solution)/shard_map/all_gather | solution.py:59
  240.5 97.8 %collective-permute-start.1 = (bf16[1024,1024]{1,0:T(8,128)(2,1)}, bf16[1024,1024]{1,0:T(8,128)(2,1)S(1)}, u32[]{:S(2)}, u32[]{:S(2)}) collective-permute-start(bf16[1024,1024]{1,0:T(8,128)(2,1)} %all-gather.15.cloned.1.call-done), channel_id=1, source_target_pairs={{0,16},{8,24},{16,32},{24,40},{32,48},{40,56},{48,64},{56,72},{64,... | collective-permute-start | bytes 6291464 | tf_op jit(solution)/shard_map/ppermute | solution.py:17
  340.5 451.4 %copy-start.1 = (bf16[128,1024]{1,0:T(8,128)(2,1)S(1)}, bf16[128,1024]{1,0:T(8,128)(2,1)}, u32[]{:S(2)}) copy-start(bf16[128,1024]{1,0:T(8,128)(2,1)} %fusion.41) | copy-start | bytes 786436
  340.5 470.0 %copy-start.2 = (bf16[128,1024]{1,0:T(8,128)(2,1)S(1)}, bf16[128,1024]{1,0:T(8,128)(2,1)}, u32[]{:S(2)}) copy-start(bf16[128,1024]{1,0:T(8,128)(2,1)} %fusion.23) | copy-start | bytes 786436
  340.5 488.3 %copy-start.3 = (bf16[128,1024]{1,0:T(8,128)(2,1)S(1)}, bf16[128,1024]{1,0:T(8,128)(2,1)}, u32[]{:S(2)}) copy-start(bf16[128,1024]{1,0:T(8,128)(2,1)} %fusion.22) | copy-start | bytes 786436
  340.5 256.6 %all-gather.19.cloned.1.call-start = ((), (), s32[]{:S(2)}) async-start(), calls=%async_computation.3 | async-start | bytes 2359296 | tf_op jit(solution)/shard_map/all_gather | solution.py:59
  373.2 190.0 %collective-permute-start.2 = (bf16[1024,1024]{1,0:T(8,128)(2,1)}, bf16[1024,1024]{1,0:T(8,128)(2,1)S(1)}, u32[]{:S(2)}, u32[]{:S(2)}) collective-permute-start(bf16[1024,1024]{1,0:T(8,128)(2,1)} %all-gather.17.cloned.1.call-done), channel_id=1, source_target_pairs={{0,32},{8,40},{16,48},{24,56},{32,64},{40,72},{48,80},{56,88},{64,... | collective-permute-start | bytes 6291464 | tf_op jit(solution)/shard_map/ppermute | solution.py:17
  597.1 258.3 %collective-permute-start.3 = (bf16[1024,1024]{1,0:T(8,128)(2,1)}, bf16[1024,1024]{1,0:T(8,128)(2,1)S(1)}, u32[]{:S(2)}, u32[]{:S(2)}) collective-permute-start(bf16[1024,1024]{1,0:T(8,128)(2,1)} %all-gather.19.cloned.1.call-done), channel_id=1, source_target_pairs={{0,64},{8,72},{16,80},{24,88},{32,96},{40,104},{48,112},{56,120},{... | collective-permute-start | bytes 6291464 | tf_op jit(solution)/shard_map/ppermute | solution.py:17
  618.5 173.4 %collective-permute-start.4 = (bf16[1024]{0:T(1024)(128)(2,1)S(1)}, bf16[1024]{0:T(1024)(128)(2,1)S(1)}, u32[]{:S(2)}, u32[]{:S(2)}) collective-permute-start(bf16[1024]{0:T(1024)(128)(2,1)S(1)} %bitcast.193), channel_id=1, source_target_pairs={{0,8},{8,16},{16,24},{24,32},{32,40},{40,48},{48,56},{56,64},{64,7... | collective-permute-start | bytes 6152 | tf_op jit(solution)/shard_map/ppermute | solution.py:17
  802.0 8.5 collective-permute-start.5
  818.5 10.3 %collective-permute-start.6 = (bf16[1024]{0:T(1024)(128)(2,1)S(1)}, bf16[1024]{0:T(1024)(128)(2,1)S(1)}, u32[]{:S(2)}, u32[]{:S(2)}) collective-permute-start(bf16[1024]{0:T(1024)(128)(2,1)S(1)} %bitcast.195), channel_id=1, source_target_pairs={{0,32},{8,40},{16,48},{24,56},{32,64},{40,72},{48,80},{56,88},{64,... | collective-permute-start | bytes 6152 | tf_op jit(solution)/shard_map/ppermute | solution.py:17
  838.7 15.1 %collective-permute-start.7 = (bf16[1024]{0:T(1024)(128)(2,1)S(1)}, bf16[1024]{0:T(1024)(128)(2,1)S(1)}, u32[]{:S(2)}, u32[]{:S(2)}) collective-permute-start(bf16[1024]{0:T(1024)(128)(2,1)S(1)} %bitcast.192), channel_id=1, source_target_pairs={{0,64},{8,72},{16,80},{24,88},{32,96},{40,104},{48,112},{56,120},{... | collective-permute-start | bytes 6152 | tf_op jit(solution)/shard_map/ppermute | solution.py:17
Sparse Core Ops, SparseCore 0:
  117.6 36.2 all-gather.12
  206.1 34.3 all-gather.14
  340.7 32.4 all-gather.16
  565.5 31.5 all-gather.18
where the time goes:
time: 872 us; the launch traced here: 864 us
  waiting for transfers between devices  656 us (75%)
  blocking collectives  89.6 us (10%)
  starting transfers between devices  35.9 us (4%)
  matrix products  34 us (4%)
  local copies, waits for them, and re-layouts  26 us (3%)
  between operations  14.5 us (2%)
    ppermute x8, waiting for transfers between devices, shifted(): return lax.ppermute(block, axis, route)  521 us
    all_gather x4, waiting for transfers between devices, shards(): lax.all_gather(matrix, 'row', axis=0, tiled=True)  135 us
    all_gather x4, blocking collectives, shards(): lax.all_gather(blocks[step], 'row', axis=0, tiled=True)  52.7 us
    all_gather x4, blocking collectives, shards(): lax.all_gather(vector.astype(jnp.bfloat16), 'row', axis=0, tiled=True)  36.9 us
    ppermute x8, starting transfers between devices, shifted(): return lax.ppermute(block, axis, route)  35.7 us
    reshape x8, local copies, waits for them, and re-layouts, sparse_rows(): grouped = piece.reshape(block_count, BS, S, BS)  23 us
  transfers between devices with their start and end apart: 12, of which 11 were waited for; matrix products, arithmetic and copies ran while one was open for 0% of the time, Pallas kernels for 0%

commit v1 on v0

v1 whole, which is shorter than its diff:
```python
import functools

import jax
import jax.numpy as jnp
from jax import lax
from jax.experimental import pallas as pl
from jax.experimental.pallas import tpu as pltpu
from jax.sharding import PartitionSpec as P

STATES = 1024
SENSORS = 128
BS = 16
S = 8
STRETCH = 4
NBLK = 64
GROUP = 8
ROWS = STATES // GROUP
STEPS = 2 * STRETCH
CHUNK = 256
PARTS = STATES // CHUNK
SPANS = (2, 4, 8)
MESH = pl.DeviceIdType.MESH
F32 = jnp.float32
BF16 = jnp.bfloat16


def dot(a, b):
    return jnp.dot(a, b, preferred_element_type=F32)


def iota(shape, axis):
    return lax.broadcasted_iota(jnp.int32, shape, axis)


def kernel(
    pattern, sensor, observations, gain, damping, blocks,
    matrix_out, vector_out,
    comp, small, damp_wide, obs_wide, pick, state, mixed, mixed_b, vector_f,
    saved, saved_v, rows_of, parts_in, vec_in, vec_row, vec_send,
    in_sem, pair_send, pair_recv, small_send, small_recv,
    c_send, c_left, c_right, c_half, c_core,
    p_send, p_left, p_right, p_half, p_core, p_in,
    swap_send, swap_recv, direct_send, up_send, vec_sends, vec_recv, out_sem,
):
    t = lax.axis_index("tm")
    i = lax.axis_index("row")
    core = i % 2
    y = i // 2
    above = ((y + 1) % 4) * 2 + core
    below = ((y + 3) % 4) * 2 + core
    opposite = ((y + 2) % 4) * 2 + core
    twin = i + 1 - 2 * core
    odd = t % 2
    pair = t + 1 - 2 * odd
    producer = [t % (2 * span) == span - 1 for span in SPANS]
    consumer = [t % (2 * span) == 2 * span - 1 for span in SPANS]
    merges = sum(c.astype(jnp.int32) for c in consumer)
    meets = merges + sum(p.astype(jnp.int32) for p in producer)

    def send(src, dst, send_sem, recv_sem, device):
        pltpu.make_async_remote_copy(
            src_ref=src, dst_ref=dst, send_sem=send_sem, recv_sem=recv_sem,
            device_id=device, device_id_type=MESH,
        ).start()

    def await_bytes(ref, sem):
        pltpu.make_async_copy(ref, ref, sem).wait()

    own_rows = pl.ds(pl.multiple_of(i * ROWS, ROWS), ROWS)
    fetch = pltpu.make_async_copy(
        blocks, comp.at[pl.ds(odd * STRETCH, STRETCH), own_rows, :], in_sem
    )
    fetch.start()

    barrier = pltpu.get_barrier_semaphore()

    def greet(device):
        pl.semaphore_signal(barrier, inc=1, device_id=device, device_id_type=MESH)

    greet((pair, i))
    for d in range(1, GROUP):
        greet((t, (i + d) % GROUP))
    for at, span in enumerate(SPANS):
        @pl.when(producer[at])
        def _():
            for j in range(GROUP):
                greet((t + span, j))

        @pl.when(consumer[at])
        def _():
            for j in range(GROUP):
                greet((t - span, j))

    small[odd] = jnp.zeros((8, STATES), F32)
    small[odd, 0:STRETCH, :] = damping[...]
    small[odd, STRETCH:8, 0:SENSORS] = observations[...].astype(F32)
    eye = iota((SENSORS, SENSORS), 0) == iota((SENSORS, SENSORS), 1)
    sensor_col = jnp.sum(
        jnp.where(eye, jnp.broadcast_to(sensor[...].astype(F32), (SENSORS, SENSORS)), 0.0),
        axis=1, keepdims=True,
    )
    pick[...] = jnp.where(
        sensor_col == iota((SENSORS, STATES), 1).astype(F32), 1.0, 0.0
    ).astype(BF16)
    first = iota((STATES, 2 * ROWS), 0) == iota((STATES, 2 * ROWS), 1) + i * ROWS
    state[...] = jnp.where(
        first & (iota((STATES, 2 * ROWS), 1) < ROWS), 1.0, 0.0
    ).astype(BF16).reshape(NBLK, BS, 2 * ROWS)
    pl.semaphore_wait(barrier, GROUP + GROUP * meets)

    def ring(buf, s_send, s_left, s_right, s_half, s_core):
        def piece(m, p, start=0, count=ROWS):
            return buf.at[m, pl.ds(pl.multiple_of(p * ROWS + start, 16), count), :]

        def begin(m):
            mine = piece(m, i)
            send(mine, mine, s_send.at[m], s_left.at[m], (t, above))
            send(mine, mine, s_send.at[m], s_right.at[m], (t, below))
            send(mine, mine, s_send.at[m], s_core.at[m], (t, twin))

        def forward(m):
            left = piece(m, below)
            await_bytes(left, s_left.at[m])
            half = piece(m, below, 0, ROWS // 2)
            send(half, half, s_send.at[m], s_half.at[m], (t, above))
            send(left, left, s_send.at[m], s_core.at[m], (t, twin))
            right = piece(m, above)
            await_bytes(right, s_right.at[m])
            half = piece(m, above, ROWS // 2, ROWS // 2)
            send(half, half, s_send.at[m], s_half.at[m], (t, below))
            send(right, right, s_send.at[m], s_core.at[m], (t, twin))

        def finish(m):
            far = piece(m, opposite)
            await_bytes(far, s_half.at[m])
            send(far, far, s_send.at[m], s_core.at[m], (t, twin))
            await_bytes(buf.at[m, pl.ds(0, 4 * ROWS), :], s_core.at[m])

        def drain(m):
            await_bytes(buf.at[m, pl.ds(0, 7 * ROWS), :], s_send.at[m])

        return begin, forward, finish, drain

    begin_c, forward_c, finish_c, drain_c = ring(comp, c_send, c_left, c_right, c_half, c_core)
    begin_p, forward_p, finish_p, drain_p = ring(parts_in, p_send, p_left, p_right, p_half, p_core)

    def start_step(n):
        @pl.when(n // STRETCH != odd)
        def _():
            await_bytes(comp.at[n, own_rows, :], pair_recv.at[n])

        begin_c(n)

    def widen(b):
        columns = jnp.transpose(small[b])
        for k in range(STRETCH):
            damp_wide[b * STRETCH + k] = jnp.broadcast_to(columns[:, k : k + 1], (STATES, ROWS))
            obs_wide[b * STRETCH + k] = jnp.broadcast_to(
                columns[:SENSORS, STRETCH + k : STRETCH + k + 1], (SENSORS, ROWS)
            )

    send(small.at[odd], small.at[odd], small_send, small_recv, (pair, i))
    fetch.wait()

    def give(k, carry):
        ref = comp.at[odd * STRETCH + k, own_rows, :]
        send(ref, ref, pair_send.at[k], pair_recv.at[odd * STRETCH + k], (pair, i))
        return carry

    lax.fori_loop(0, STRETCH, give, 0)
    start_step(0)
    start_step(1)
    widen(odd)
    start_step(2)
    start_step(3)
    forward_c(0)
    await_bytes(small.at[1 - odd], small_recv)
    widen(1 - odd)
    forward_c(1)

    def step(n, carry):
        @pl.when(n + 4 < STEPS)
        def _():
            start_step(n + 4)

        @pl.when(n + 2 < STEPS)
        def _():
            forward_c(n + 2)

        finish_c(n)
        for part in range(GROUP):
            rows = slice(part * ROWS, (part + 1) * ROWS)
            products = []
            for r in range(part * GROUP, (part + 1) * GROUP):
                chosen = jnp.concatenate(
                    [
                        state[pattern[r, s]] for s in range(S)
                    ],
                    axis=0,
                )
                products.append(dot(comp[n, r * BS : (r + 1) * BS, :], chosen))
            wide = damp_wide[n, rows, :]
            value = state[part * GROUP : (part + 1) * GROUP].reshape(ROWS, 2 * ROWS).astype(F32) * jnp.concatenate([wide, wide], axis=1)
            value = value + jnp.concatenate(products, axis=0)
            mixed[rows, :] = value
            mixed_b[rows, :] = value.astype(BF16)
        quarter = STATES // 4
        seen = sum(
            dot(pick[:, q * quarter : (q + 1) * quarter], mixed_b[q * quarter : (q + 1) * quarter, :])
            for q in range(4)
        )
        lane = iota((SENSORS, ROWS), 1)
        readings = jnp.where(lane == 0, obs_wide[n], 0.0)
        seen = jnp.concatenate([seen[:, :ROWS], seen[:, ROWS:] - readings], axis=1).astype(BF16)
        for q in range(4):
            rows = slice(q * quarter, (q + 1) * quarter)
            value = mixed[rows, :] - dot(gain[rows, :], seen)
            state[q * 16 : (q + 1) * 16] = value.astype(BF16).reshape(16, BS, 2 * ROWS)
            vector_f[rows, :] = value[:, ROWS:]

        @pl.when(n == (1 + odd) * STRETCH - 1)
        def _():
            saved[...] = state[:, :, 0:ROWS].reshape(STATES, ROWS)
            saved_v[...] = vector_f[own_rows, :]

        return carry

    lax.fori_loop(0, STEPS, step, 0)

    def block(j):
        return saved.at[pl.ds(pl.multiple_of(j * ROWS, ROWS), ROWS), :]

    own_columns = pl.ds(pl.multiple_of(i * ROWS, ROWS), ROWS)

    @pl.when(producer[0])
    def _():
        lanes = pl.ds(pl.multiple_of((i % 2) * ROWS, ROWS), ROWS)
        for d in range(GROUP):
            j = (i + d) % GROUP
            rows = pl.ds(pl.multiple_of(j * ROWS, ROWS), ROWS)
            send(
                block(j), parts_in.at[i // 2, rows, lanes], direct_send, p_in.at[i // 2],
                (t + SPANS[0], j),
            )

    for d in range(1, GROUP):
        j = (i + d) % GROUP
        send(block(j), rows_of.at[0, :, own_columns], swap_send, swap_recv, (t, j))
    rows_of[0, :, own_columns] = saved[own_rows, :]
    vec_row[...] = jnp.transpose(saved_v[...])[0:8, :]

    def give_vector(level):
        value = vec_row[0:1, :]
        high = value.astype(BF16)
        low = (value - high.astype(F32)).astype(BF16)
        row = iota((16, ROWS), 0)
        both = jnp.where(
            row == 0, jnp.broadcast_to(high.astype(F32), (16, ROWS)),
            jnp.where(row == 1, jnp.broadcast_to(low.astype(F32), (16, ROWS)), 0.0),
        )
        vec_send[level] = both.astype(BF16)
        for j in range(GROUP):
            send(
                vec_send.at[level], vec_in.at[level, :, own_columns],
                vec_sends.at[level], vec_recv.at[level], (t + SPANS[level], j),
            )

    @pl.when(producer[0])
    def _():
        give_vector(0)

    def start_part(m):
        await_bytes(parts_in.at[m, own_rows, :], p_in.at[m])
        begin_p(m)

    count = PARTS * merges

    @pl.when(merges > 0)
    def _():
        start_part(0)
        start_part(1)
        forward_p(0)

    await_bytes(rows_of.at[0, :, pl.ds(0, 7 * ROWS)], swap_recv)

    def merge(m, carry):
        @pl.when(m + 2 < count)
        def _():
            start_part(m + 2)

        @pl.when(m + 1 < count)
        def _():
            forward_p(m + 1)

        finish_p(m)
        level = m // PARTS
        part = m % PARTS
        columns = pl.ds(pl.multiple_of(part * CHUNK, CHUNK), CHUNK)
        rows_of[level + 1, :, columns] = dot(rows_of[level], parts_in[m]).astype(BF16)
        for at in (1, 2):
            @pl.when(producer[at] & (level == at - 1))
            def _():
                send(
                    rows_of.at[level + 1, :, columns], parts_in.at[m + PARTS, own_rows, :],
                    up_send.at[part], p_in.at[m + PARTS], (t + SPANS[at], i),
                )

        @pl.when(part == 1)
        def _():
            await_bytes(vec_in.at[level], vec_recv.at[level])
            found = lax.dot_general(
                vec_in[level], rows_of[level], (((1,), (1,)), ((), ())),
                preferred_element_type=F32,
            )
            vec_row[0:1, :] = vec_row[0:1, :] + found[0:1, :] + found[1:2, :]
            for at in (1, 2):
                @pl.when(producer[at] & (level == at - 1))
                def _():
                    give_vector(at)

        return carry

    lax.fori_loop(0, count, merge, 0)

    result = pltpu.make_async_copy(rows_of.at[merges], matrix_out.at[0], out_sem)
    result.start()
    vector_out[...] = vec_row[0:1, :]

    def drained(n, carry):
        drain_c(n)
        return carry

    lax.fori_loop(0, STEPS, drained, 0)

    def given(k, carry):
        await_bytes(comp.at[odd * STRETCH + k, own_rows, :], pair_send.at[k])
        return carry

    lax.fori_loop(0, STRETCH, given, 0)
    await_bytes(small.at[odd], small_send)
    await_bytes(rows_of.at[0, :, pl.ds(0, 7 * ROWS)], swap_send)

    def drained_part(m, carry):
        drain_p(m)
        return carry

    lax.fori_loop(0, count, drained_part, 0)

    @pl.when(producer[0])
    def _():
        await_bytes(saved, direct_send)

    @pl.when(producer[1] | producer[2])
    def _():
        for part in range(PARTS):
            await_bytes(parts_in.at[0, own_rows, :], up_send.at[part])

    for at in range(3):
        @pl.when(producer[at])
        def _():
            await_bytes(vec_in.at[at], vec_sends.at[at])

    result.wait()


def shards(observations, gain, damping, blocks, pattern, sensor_index):
    vmem = pl.BlockSpec(memory_space=pltpu.VMEM)
    dma = pltpu.SemaphoreType.DMA
    merges = len(SPANS)
    moves = PARTS * merges
    return pl.pallas_call(
        kernel,
        out_shape=(
            jax.ShapeDtypeStruct((1, ROWS, STATES), BF16),
            jax.ShapeDtypeStruct((1, ROWS), F32),
        ),
        in_specs=[
            pl.BlockSpec(memory_space=pltpu.SMEM), vmem, vmem, vmem, vmem,
            pl.BlockSpec(memory_space=pl.ANY),
        ],
        out_specs=(pl.BlockSpec(memory_space=pl.ANY), vmem),
        scratch_shapes=[
            pltpu.VMEM((STEPS, STATES, SENSORS), BF16),
            pltpu.VMEM((2, 8, STATES), F32),
            pltpu.VMEM((STEPS, STATES, ROWS), F32),
            pltpu.VMEM((STEPS, SENSORS, ROWS), F32),
            pltpu.VMEM((SENSORS, STATES), BF16),
            pltpu.VMEM((NBLK, BS, 2 * ROWS), BF16),
            pltpu.VMEM((STATES, 2 * ROWS), F32),
            pltpu.VMEM((STATES, 2 * ROWS), BF16),
            pltpu.VMEM((STATES, ROWS), F32),
            pltpu.VMEM((STATES, ROWS), BF16),
            pltpu.VMEM((ROWS, ROWS), F32),
            pltpu.VMEM((merges + 1, ROWS, STATES), BF16),
            pltpu.VMEM((moves, STATES, CHUNK), BF16),
            pltpu.VMEM((merges, 16, STATES), BF16),
            pltpu.VMEM((8, ROWS), F32),
            pltpu.VMEM((merges, 16, ROWS), BF16),
            dma, dma((STRETCH,)), dma((STEPS,)), dma, dma,
            dma((STEPS,)), dma((STEPS,)), dma((STEPS,)), dma((STEPS,)), dma((STEPS,)),
            dma((moves,)), dma((moves,)), dma((moves,)), dma((moves,)), dma((moves,)), dma((moves,)),
            dma, dma, dma, dma((PARTS,)), dma((merges,)), dma((merges,)), dma,
        ],
        compiler_params=pltpu.CompilerParams(
            collective_id=0, has_side_effects=True, vmem_limit_bytes=48 * 2**20
        ),
    )(pattern, sensor_index.reshape(1, SENSORS), observations, gain, damping, blocks)


def solution(mesh):
    return jax.shard_map(
        shards,
        mesh=mesh,
        in_specs=(P("tm", None), P(), P("tm", None), P("tm", "row", None), P(), P()),
        out_specs=(P("tm", "row", None), P("tm", "row")),
        check_vma=False,
    )
```

time: 872 us -> 93.1 us (0.11)
  the two profiles are of different devices: /device:TPU:36 before, /device:TPU:481 now
where the time goes in v1:
time: 93.1 us; the launch traced here: 92.8 us
  Pallas kernels  88.3 us (95%)
  local copies, waits for them, and re-layouts  3.86 us (4%)
    pallas_call x1, Pallas kernels, shards(): pl.pallas_call(kernel, out_shape=(jax.ShapeDtypeStruct((1, ROWS, STATES),...  88.3 us
    unnamed x13, local copies, waits for them, and re-layouts  3.86 us

profile of v1, /device:TPU:481, one launch (start us, length us, event | category | flops | bytes accessed | tf_op | source)
XLA Modules:
  0.0 92.8 jit_solution(2691398031733711717)
XLA Ops:
  0.6 0.0 copy-start.2
  0.6 0.0 copy-start.3
  0.7 0.0 copy-start.4
  0.7 0.8 copy.8.pattern
  1.4 0.0 copy-done.2
  1.5 0.0 copy-done.3
  1.5 0.0 copy-done.4
  1.5 0.0 copy-start
  1.5 0.9 %copy-done = bf16[1024,128]{1,0:T(8,128)(2,1)S(1)} copy-done((bf16[1024,128]{1,0:T(8,128)(2,1)S(1)}, bf16[1024,128]{1,0:T(8,128)(2,1)}, u32[]{:S(2)}) %copy-start) | copy-done | bytes 262168
  2.4 0.0 copy-start.1
  2.4 0.9 copy-done.1
  3.3 88.3 %shard_map.77 = (bf16[1,128,1024]{2,1,0:T(8,128)(2,1)S(1)}, f32[1,128]{1,0:T(1,128)S(1)}) custom-call(s32[64,8]{1,0:T(8,128)S(1)} %copy.8.pattern, s32[1,128]{1,0:T(1,128)S(1)} %bitcast.1, bf16[4,128]{1,0:T(4,128)(2,1)S(1)} %copy-done.3, bf16[1024,128]{1,0:T(8,128)(2,1)S(1)} %copy-done, f32[4,1024]{1,0:T(4,128)S(1)} %copy-done.2, ...), custom_call_target="tpu_custom_call" | custom-call | tf_op jit(solution)/shard_map/pallas_call | solution.py:371
  91.6 0.7 copy.11
  92.3 0.5 copy.12
Async XLA Ops:
  0.6 0.8 copy-start.2
  0.6 0.8 copy-start.3
  0.7 0.8 copy-start.4
  1.5 1.0 %copy-start = (bf16[1024,128]{1,0:T(8,128)(2,1)S(1)}, bf16[1024,128]{1,0:T(8,128)(2,1)}, u32[]{:S(2)}) copy-start(bf16[1024,128]{1,0:T(8,128)(2,1)} %gain.1) | copy-start | bytes 786436
  2.4 0.9 copy-start.1

commit v2 on v1

v2 whole, which is shorter than its diff:
```python
import functools

import jax
import jax.numpy as jnp
from jax import lax
from jax.experimental import pallas as pl
from jax.experimental.pallas import tpu as pltpu
from jax.sharding import PartitionSpec as P

STATES = 1024
SENSORS = 128
BS = 16
S = 8
STRETCH = 4
NBLK = 64
GROUP = 8
ROWS = STATES // GROUP
STEPS = 2 * STRETCH
CHUNK = 256
PARTS = STATES // CHUNK
SPANS = (2, 4, 8)
MESH = pl.DeviceIdType.MESH
F32 = jnp.float32
BF16 = jnp.bfloat16


def dot(a, b):
    return jnp.dot(a, b, preferred_element_type=F32)


def iota(shape, axis):
    return lax.broadcasted_iota(jnp.int32, shape, axis)


def kernel(
    pattern, sensor, observations, gain, damping, blocks,
    matrix_out, vector_out,
    comp, small, damp_wide, obs_wide, pick, state, mixed, mixed_b, vector_f,
    columns_of, whole, earlier, vec_in, vec_row, vec_send, rows_out,
    in_sem, small_send, small_recv,
    c_send, c_twin, c_mine, c_left, c_right, c_far, c_core,
    m_send, m_twin, m_left, m_right, m_far, m_core,
    up_send, up_recv, vec_sends, vec_recv, swap_send, swap_recv, out_sem,
):
    t = lax.axis_index("tm")
    i = lax.axis_index("row")
    core = i % 2
    y = i // 2
    above = ((y + 1) % 4) * 2 + core
    below = ((y + 3) % 4) * 2 + core
    opposite = ((y + 2) % 4) * 2 + core
    twin = i + 1 - 2 * core
    odd = t % 2
    pair = t + 1 - 2 * odd
    producer = [t % (2 * span) == span - 1 for span in SPANS]
    consumer = [t % (2 * span) == 2 * span - 1 for span in SPANS]
    merges = sum(c.astype(jnp.int32) for c in consumer)
    meets = merges + sum(p.astype(jnp.int32) for p in producer)
    count = PARTS * merges

    def send(src, dst, send_sem, recv_sem, device):
        pltpu.make_async_remote_copy(
            src_ref=src, dst_ref=dst, send_sem=send_sem, recv_sem=recv_sem,
            device_id=device, device_id_type=MESH,
        ).start()

    def await_bytes(ref, sem):
        pltpu.make_async_copy(ref, ref, sem).wait()

    def span_of(p, size=ROWS):
        return pl.ds(pl.multiple_of(p * size, size), size)

    own = span_of(i)
    fetch = pltpu.make_async_copy(
        blocks, comp.at[pl.ds(odd * STRETCH, STRETCH), own, :], in_sem
    )
    fetch.start()

    barrier = pltpu.get_barrier_semaphore()

    def greet(device):
        pl.semaphore_signal(barrier, inc=1, device_id=device, device_id_type=MESH)

    for j in (i, above, below, opposite):
        greet((pair, j))
    for d in range(1, GROUP):
        greet((t, (i + d) % GROUP))
    for at, span in enumerate(SPANS):
        @pl.when(producer[at])
        def _():
            greet((t + span, i))

        @pl.when(consumer[at])
        def _():
            greet((t - span, i))

    small[odd] = jnp.zeros((8, STATES), F32)
    small[odd, 0:STRETCH, :] = damping[...]
    small[odd, STRETCH:8, 0:SENSORS] = observations[...].astype(F32)
    eye = iota((SENSORS, SENSORS), 0) == iota((SENSORS, SENSORS), 1)
    sensor_col = jnp.sum(
        jnp.where(eye, jnp.broadcast_to(sensor[...].astype(F32), (SENSORS, SENSORS)), 0.0),
        axis=1, keepdims=True,
    )
    pick[...] = jnp.where(
        sensor_col == iota((SENSORS, STATES), 1).astype(F32), 1.0, 0.0
    ).astype(BF16)
    first = iota((STATES, 2 * ROWS), 0) == iota((STATES, 2 * ROWS), 1) + i * ROWS
    state[...] = jnp.where(
        first & (iota((STATES, 2 * ROWS), 1) < ROWS), 1.0, 0.0
    ).astype(BF16).reshape(NBLK, BS, 2 * ROWS)
    pl.semaphore_wait(barrier, GROUP + 3 + meets)

    def piece(n, p):
        return comp.at[n, span_of(p), :]

    def give_step(n):
        mine = piece(n, i)
        for group in (t, pair):
            send(mine, mine, c_send.at[n], c_far.at[n], (group, opposite))
            send(mine, mine, c_send.at[n], c_left.at[n], (group, above))
            send(mine, mine, c_send.at[n], c_right.at[n], (group, below))
        send(mine, mine, c_send.at[n], c_mine.at[n], (pair, i))
        send(mine, mine, c_twin.at[n], c_core.at[n], (t, twin))

    def pass_step(n):
        @pl.when(n // STRETCH != odd)
        def _():
            mine = piece(n, i)
            await_bytes(mine, c_mine.at[n])
            send(mine, mine, c_twin.at[n], c_core.at[n], (t, twin))

        for p, sems in ((below, c_left), (above, c_right), (opposite, c_far)):
            part = piece(n, p)
            await_bytes(part, sems.at[n])
            send(part, part, c_twin.at[n], c_core.at[n], (t, twin))

    def widen(b):
        columns = jnp.transpose(small[b])
        for k in range(STRETCH):
            damp_wide[b * STRETCH + k] = jnp.broadcast_to(columns[:, k : k + 1], (STATES, ROWS))
            obs_wide[b * STRETCH + k] = jnp.broadcast_to(
                columns[:SENSORS, STRETCH + k : STRETCH + k + 1], (SENSORS, ROWS)
            )

    fetch.wait()

    @pl.when(odd == 0)
    def _():
        give_step(0)

    send(small.at[odd], small.at[odd], small_send, small_recv, (pair, i))

    @pl.when(odd == 0)
    def _():
        def give(k, carry):
            give_step(k)
            return carry

        lax.fori_loop(1, STRETCH, give, 0)

    widen(odd)
    await_bytes(small.at[1 - odd], small_recv)
    widen(1 - odd)
    pass_step(0)

    @pl.when(odd == 1)
    def _():
        give_step(STRETCH)

    def step(n, carry):
        @pl.when((odd == 1) & (n < STRETCH - 1))
        def _():
            give_step(n + STRETCH + 1)

        @pl.when(n + 1 < STEPS)
        def _():
            pass_step(n + 1)

        await_bytes(comp.at[n, pl.ds(0, 4 * ROWS), :], c_core.at[n])
        for part in range(GROUP):
            rows = slice(part * ROWS, (part + 1) * ROWS)
            products = []
            for r in range(part * GROUP, (part + 1) * GROUP):
                chosen = jnp.concatenate([state[pattern[r, s]] for s in range(S)], axis=0)
                products.append(dot(comp[n, r * BS : (r + 1) * BS, :], chosen))
            wide = damp_wide[n, rows, :]
            old = state[part * GROUP : (part + 1) * GROUP].reshape(ROWS, 2 * ROWS)
            value = old.astype(F32) * jnp.concatenate([wide, wide], axis=1)
            value = value + jnp.concatenate(products, axis=0)
            mixed[rows, :] = value
            mixed_b[rows, :] = value.astype(BF16)
        quarter = STATES // 4
        seen = sum(
            dot(pick[:, q * quarter : (q + 1) * quarter], mixed_b[q * quarter : (q + 1) * quarter, :])
            for q in range(4)
        )
        lane = iota((SENSORS, ROWS), 1)
        readings = jnp.where(lane == 0, obs_wide[n], 0.0)
        seen = jnp.concatenate([seen[:, :ROWS], seen[:, ROWS:] - readings], axis=1).astype(BF16)
        for q in range(4):
            rows = slice(q * quarter, (q + 1) * quarter)
            value = mixed[rows, :] - dot(gain[rows, :], seen)
            state[q * 16 : (q + 1) * 16] = value.astype(BF16).reshape(16, BS, 2 * ROWS)
            vector_f[rows, :] = value[:, ROWS:]

        @pl.when(n == (1 + odd) * STRETCH - 1)
        def _():
            columns_of[0] = state[:, :, 0:ROWS].reshape(STATES, ROWS)
            for part in range(GROUP):
                rows = slice(part * ROWS, (part + 1) * ROWS)
                vec_row[0:1, rows] = jnp.transpose(vector_f[rows, :])[0:1, :]

        return carry

    lax.fori_loop(0, STEPS, step, 0)

    def rows_at(m):
        return span_of(m % PARTS, CHUNK)

    def give_vector(level):
        value = vec_row[0:1, :]
        high = value.astype(BF16).astype(F32)
        row = iota((16, STATES), 0)
        both = jnp.where(
            row == 0, jnp.broadcast_to(high, (16, STATES)),
            jnp.where(row == 1, jnp.broadcast_to(value - high, (16, STATES)), 0.0),
        )
        vec_send[...] = both.astype(BF16)
        send(vec_send, vec_in.at[level], vec_sends, vec_recv.at[level], (t + SPANS[level], i))

    def give_up(level, m):
        rows = rows_at(m)
        send(
            columns_of.at[level, rows, :], earlier.at[level, rows, :],
            up_send.at[m % PARTS], up_recv.at[level * PARTS + m % PARTS], (t + SPANS[level], i),
        )

    def give_part(m):
        level = m // PARTS
        rows = rows_at(m)
        src = columns_of.at[level, rows, :]
        dst = whole.at[level, rows, own]
        send(src, dst, m_send.at[m], m_far.at[m], (t, opposite))
        send(src, dst, m_send.at[m], m_left.at[m], (t, above))
        send(src, dst, m_send.at[m], m_right.at[m], (t, below))
        send(src, dst, m_twin.at[m], m_core.at[m], (t, twin))
        whole[level, rows, own] = columns_of[level, rows, :]

    def pass_part(m):
        for p, sems in ((below, m_left), (above, m_right), (opposite, m_far)):
            part = whole.at[m // PARTS, rows_at(m), span_of(p)]
            await_bytes(part, sems.at[m])
            send(part, part, m_twin.at[m], m_core.at[m], (t, twin))

    @pl.when(producer[0])
    def _():
        for m in range(PARTS):
            give_up(0, m)
        give_vector(0)

    @pl.when(merges > 0)
    def _():
        def give(m, carry):
            give_part(m)
            return carry

        lax.fori_loop(0, PARTS, give, 0)
        pass_part(0)

    def merge(m, carry):
        @pl.when(m + 1 < count)
        def _():
            pass_part(m + 1)

        level = m // PARTS
        rows = rows_at(m)

        @pl.when(m % PARTS == 0)
        def _():
            for q in range(PARTS):
                await_bytes(
                    earlier.at[level, pl.ds(q * CHUNK, CHUNK), :], up_recv.at[level * PARTS + q]
                )

        await_bytes(whole.at[level, rows, pl.ds(0, 4 * ROWS)], m_core.at[m])
        columns_of[level + 1, rows, :] = dot(whole[level, rows, :], earlier[level]).astype(BF16)

        @pl.when(m + PARTS < count)
        def _():
            give_part(m + PARTS)

        for at in (1, 2):
            @pl.when(producer[at] & (level == at - 1))
            def _():
                give_up(at, m)

        @pl.when(m % PARTS == PARTS - 1)
        def _():
            await_bytes(vec_in.at[level], vec_recv.at[level])
            found = lax.dot_general(
                vec_in[level], whole[level], (((1,), (1,)), ((), ())),
                preferred_element_type=F32,
            )
            vec_row[0:1, :] = vec_row[0:1, :] + found[0:1, :] + found[1:2, :]
            for at in (1, 2):
                @pl.when(producer[at] & (level == at - 1))
                def _():
                    give_vector(at)

        return carry

    lax.fori_loop(0, count, merge, 0)

    for d in (4, 5, 3, 2, 6, 7, 1):
        j = (i + d) % GROUP
        send(
            columns_of.at[merges, span_of(j), :], rows_out.at[:, own], swap_send, swap_recv, (t, j)
        )
    rows_out[:, own] = columns_of[merges, own, :]
    vector_out[...] = vec_row[0:1, own]

    def drained(n, carry):
        await_bytes(comp.at[n, pl.ds(0, 4 * ROWS), :], c_twin.at[n])
        return carry

    lax.fori_loop(0, STEPS, drained, 0)

    def drained_own(k, carry):
        n = odd * STRETCH + k
        await_bytes(comp.at[n, pl.ds(0, 7 * ROWS), :], c_send.at[n])
        return carry

    lax.fori_loop(0, STRETCH, drained_own, 0)
    await_bytes(small.at[odd], small_send)

    def drained_part(m, carry):
        rows = rows_at(m)
        await_bytes(whole.at[m // PARTS, rows, pl.ds(0, 3 * ROWS)], m_send.at[m])
        await_bytes(whole.at[m // PARTS, rows, pl.ds(0, 4 * ROWS)], m_twin.at[m])
        return carry

    lax.fori_loop(0, count, drained_part, 0)

    @pl.when(producer[0] | producer[1] | producer[2])
    def _():
        for q in range(PARTS):
            await_bytes(earlier.at[0, pl.ds(q * CHUNK, CHUNK), :], up_send.at[q])
        await_bytes(vec_send, vec_sends)

    await_bytes(rows_out.at[:, pl.ds(0, 7 * ROWS)], swap_recv)
    result = pltpu.make_async_copy(rows_out, matrix_out.at[0], out_sem)
    result.start()
    await_bytes(rows_out.at[:, pl.ds(0, 7 * ROWS)], swap_send)
    result.wait()


def shards(observations, gain, damping, blocks, pattern, sensor_index):
    vmem = pl.BlockSpec(memory_space=pltpu.VMEM)
    dma = pltpu.SemaphoreType.DMA
    merges = len(SPANS)
    moves = PARTS * merges
    return pl.pallas_call(
        kernel,
        out_shape=(
            jax.ShapeDtypeStruct((1, ROWS, STATES), BF16),
            jax.ShapeDtypeStruct((1, ROWS), F32),
        ),
        in_specs=[
            pl.BlockSpec(memory_space=pltpu.SMEM), vmem, vmem, vmem, vmem,
            pl.BlockSpec(memory_space=pl.ANY),
        ],
        out_specs=(pl.BlockSpec(memory_space=pl.ANY), vmem),
        scratch_shapes=[
            pltpu.VMEM((STEPS, STATES, SENSORS), BF16),
            pltpu.VMEM((2, 8, STATES), F32),
            pltpu.VMEM((STEPS, STATES, ROWS), F32),
            pltpu.VMEM((STEPS, SENSORS, ROWS), F32),
            pltpu.VMEM((SENSORS, STATES), BF16),
            pltpu.VMEM((NBLK, BS, 2 * ROWS), BF16),
            pltpu.VMEM((STATES, 2 * ROWS), F32),
            pltpu.VMEM((STATES, 2 * ROWS), BF16),
            pltpu.VMEM((STATES, ROWS), F32),
            pltpu.VMEM((merges + 1, STATES, ROWS), BF16),
            pltpu.VMEM((merges, STATES, STATES), BF16),
            pltpu.VMEM((merges, STATES, ROWS), BF16),
            pltpu.VMEM((merges, 16, STATES), BF16),
            pltpu.VMEM((8, STATES), F32),
            pltpu.VMEM((16, STATES), BF16),
            pltpu.VMEM((ROWS, STATES), BF16),
            dma, dma, dma,
            *[dma((STEPS,))] * 7,
            *[dma((moves,))] * 6,
            dma((PARTS,)), dma((moves,)), dma, dma((merges,)), dma, dma, dma,
        ],
        compiler_params=pltpu.CompilerParams(
            collective_id=0, has_side_effects=True, vmem_limit_bytes=48 * 2**20
        ),
    )(pattern, sensor_index.reshape(1, SENSORS), observations, gain, damping, blocks)


def solution(mesh):
    return jax.shard_map(
        shards,
        mesh=mesh,
        in_specs=(P("tm", None), P(), P("tm", None), P("tm", "row", None), P(), P()),
        out_specs=(P("tm", "row", None), P("tm", "row")),
        check_vma=False,
    )
```

time: 93.1 us -> 76.8 us (0.82)
  Pallas kernels: 88.3 us -> 71.6 us
    pallas_call x1, Pallas kernels: 88.3 us -> 71.6 us  [shards(): pl.pallas_call(kernel, out_shape=(jax.ShapeDtypeStruct((1, ROWS, STATES),...]
where the time goes in v2:
time: 76.8 us; the launch traced here: 76.2 us
  Pallas kernels  71.6 us (93%)
  local copies, waits for them, and re-layouts  3.86 us (5%)
    pallas_call x1, Pallas kernels, shards(): pl.pallas_call(kernel, out_shape=(jax.ShapeDtypeStruct((1, ROWS, STATES),...  71.6 us
    unnamed x13, local copies, waits for them, and re-layouts  3.86 us

profile of v2, /device:TPU:481, one launch (start us, length us, event | category | flops | bytes accessed | tf_op | source)
XLA Modules:
  0.0 76.2 jit_solution(9530197437081974825)
XLA Ops:
  0.6 0.0 copy-start.2
  0.6 0.0 copy-start.3
  0.7 0.0 copy-start.4
  0.7 0.8 %copy.8.pattern = s32[64,8]{1,0:T(8,128)S(1)} copy(s32[64,8]{0,1:T(8,128)} %param.10) | data formatting | bytes 4096 | tf_op args[4]
  1.4 0.0 copy-done.2
  1.5 0.0 copy-done.3
  1.5 0.0 copy-done.4
  1.5 0.0 copy-start
  1.5 0.9 %copy-done = bf16[1024,128]{1,0:T(8,128)(2,1)S(1)} copy-done((bf16[1024,128]{1,0:T(8,128)(2,1)S(1)}, bf16[1024,128]{1,0:T(8,128)(2,1)}, u32[]{:S(2)}) %copy-start) | copy-done | bytes 262168
  2.4 0.0 copy-start.1
  2.4 0.9 %copy-done.1 = bf16[4,128,128]{2,1,0:T(8,128)(2,1)S(1)} copy-done((bf16[4,128,128]{2,1,0:T(8,128)(2,1)S(1)}, bf16[4,128,128]{2,1,0:T(8,128)(2,1)}, u32[]{:S(2)}) %copy-start.1) | copy-done | bytes 131096
  3.3 71.6 %shard_map.77 = (bf16[1,128,1024]{2,1,0:T(8,128)(2,1)S(1)}, f32[1,128]{1,0:T(1,128)S(1)}) custom-call(s32[64,8]{1,0:T(8,128)S(1)} %copy.8.pattern, s32[1,128]{1,0:T(1,128)S(1)} %bitcast.1, bf16[4,128]{1,0:T(4,128)(2,1)S(1)} %copy-done.3, bf16[1024,128]{1,0:T(8,128)(2,1)S(1)} %copy-done, f32[4,1024]{1,0:T(4,128)S(1)} %copy-done.2, ...), custom_call_target="tpu_custom_call" | custom-call | tf_op jit(solution)/shard_map/pallas_call | solution.py:363
  74.9 0.7 copy.11
  75.6 0.5 copy.12
Async XLA Ops:
  0.6 0.8 %copy-start.2 = (f32[4,1024]{1,0:T(4,128)S(1)}, f32[4,1024]{1,0:T(4,128)}, u32[]{:S(2)}) copy-start(f32[4,1024]{1,0:T(4,128)} %damping.1) | copy-start | bytes 49156
  0.6 0.8 %copy-start.3 = (bf16[4,128]{1,0:T(4,128)(2,1)S(1)}, bf16[4,128]{1,0:T(4,128)(2,1)}, u32[]{:S(2)}) copy-start(bf16[4,128]{1,0:T(4,128)(2,1)} %observations.1) | copy-start | bytes 3076
  0.7 0.8 %copy-start.4 = (s32[128]{0:T(128)S(1)}, s32[128]{0:T(128)}, u32[]{:S(2)}) copy-start(s32[128]{0:T(128)} %param.11) | copy-start | bytes 1540
  1.5 1.0 %copy-start = (bf16[1024,128]{1,0:T(8,128)(2,1)S(1)}, bf16[1024,128]{1,0:T(8,128)(2,1)}, u32[]{:S(2)}) copy-start(bf16[1024,128]{1,0:T(8,128)(2,1)} %gain.1) | copy-start | bytes 786436
  2.4 0.9 %copy-start.1 = (bf16[4,128,128]{2,1,0:T(8,128)(2,1)S(1)}, bf16[4,128,128]{2,1,0:T(8,128)(2,1)}, u32[]{:S(2)}) copy-start(bf16[4,128,128]{2,1,0:T(8,128)(2,1)} %blocks.1) | copy-start | bytes 393220

commit v3 on v2

v3 whole, which is shorter than its diff:
```python
import functools

import jax
import jax.numpy as jnp
from jax import lax
from jax.experimental import pallas as pl
from jax.experimental.pallas import tpu as pltpu
from jax.sharding import PartitionSpec as P

STATES = 1024
SENSORS = 128
BS = 16
S = 8
STRETCH = 4
NBLK = 64
GROUP = 8
ROWS = STATES // GROUP
STEPS = 2 * STRETCH
CHUNK = 256
PARTS = STATES // CHUNK
PACE = 4
SPANS = (2, 4, 8)
VMEM_BYTES = 63 * 2**20
MESH = pl.DeviceIdType.MESH
F32 = jnp.float32
BF16 = jnp.bfloat16


def dot(a, b):
    return jnp.dot(a, b, preferred_element_type=F32)


def iota(shape, axis):
    return lax.broadcasted_iota(jnp.int32, shape, axis)


def kernel(
    pattern_in, sensor_in, observations_in, gain_in, damping_in, blocks,
    matrix_out, vector_out,
    pattern, sensor, observations, gain, damping,
    comp, small, damp_wide, obs_wide, pick, state, mixed, mixed_b, vector_f,
    columns_of, whole, earlier, vec_in, vec_row, vec_send, rows_out,
    in_sems, small_send, small_recv,
    c_send, c_over, c_twin, c_mine, c_left, c_right, c_far, c_core,
    m_send, m_twin, m_left, m_right, m_far, m_core,
    up_send, up_recv, vec_sends, vec_recv, swap_send, swap_recv, out_sem,
):
    t = lax.axis_index("tm")
    i = lax.axis_index("row")
    core = i % 2
    y = i // 2
    above = ((y + 1) % 4) * 2 + core
    below = ((y + 3) % 4) * 2 + core
    opposite = ((y + 2) % 4) * 2 + core
    twin = i + 1 - 2 * core
    odd = t % 2
    lead = t - odd + 1
    producer = [t % (2 * span) == span - 1 for span in SPANS]
    consumer = [t % (2 * span) == 2 * span - 1 for span in SPANS]
    merges = sum(c.astype(jnp.int32) for c in consumer)
    meets = sum(p.astype(jnp.int32) for p in producer)
    count = PARTS * merges

    def send(src, dst, send_sem, recv_sem, device):
        pltpu.make_async_remote_copy(
            src_ref=src, dst_ref=dst, send_sem=send_sem, recv_sem=recv_sem,
            device_id=device, device_id_type=MESH,
        ).start()

    def await_bytes(ref, sem):
        pltpu.make_async_copy(ref, ref, sem).wait()

    def span_of(p, size=ROWS):
        return pl.ds(pl.multiple_of(p * size, size), size)

    own = span_of(i)
    fetches = [
        pltpu.make_async_copy(src, dst, in_sems.at[k])
        for k, (src, dst) in enumerate(
            (
                (blocks, comp.at[pl.ds(odd * STRETCH, STRETCH), own, :]),
                (damping_in, damping), (observations_in, observations),
                (sensor_in, sensor), (pattern_in, pattern), (gain_in, gain),
            )
        )
    ]
    for fetch in fetches:
        fetch.start()
    barrier = pltpu.get_barrier_semaphore()

    def greet(device):
        pl.semaphore_signal(barrier, inc=1, device_id=device, device_id_type=MESH)

    for at, span in enumerate(SPANS):
        @pl.when(consumer[at])
        def _():
            greet((t - span, i))

    @pl.when(odd == 1)
    def _():
        greet((t - 1, i))

    for d in range(1, GROUP):
        greet((t, (i + d) % GROUP))

    for fetch in fetches[1:3]:
        fetch.wait()
    small[odd] = jnp.zeros((8, STATES), F32)
    small[odd, 0:STRETCH, :] = damping[...]
    small[odd, STRETCH:8, 0:SENSORS] = observations[...].astype(F32)
    for fetch in fetches[3:5]:
        fetch.wait()

    def widen(b):
        columns = jnp.transpose(small[b])
        for k in range(STRETCH):
            damp_wide[b * STRETCH + k] = jnp.broadcast_to(columns[:, k : k + 1], (STATES, ROWS))
            obs_wide[b * STRETCH + k] = jnp.broadcast_to(
                columns[:SENSORS, STRETCH + k : STRETCH + k + 1], (SENSORS, ROWS)
            )

    if True:
        eye = iota((SENSORS, SENSORS), 0) == iota((SENSORS, SENSORS), 1)
        sensor_col = jnp.sum(
            jnp.where(eye, jnp.broadcast_to(sensor[...].astype(F32), (SENSORS, SENSORS)), 0.0),
            axis=1, keepdims=True,
        )
        pick[...] = jnp.where(
            sensor_col == iota((SENSORS, STATES), 1).astype(F32), 1.0, 0.0
        ).astype(BF16)
        first = iota((STATES, 2 * ROWS), 0) == iota((STATES, 2 * ROWS), 1) + i * ROWS
        state[...] = jnp.where(
            first & (iota((STATES, 2 * ROWS), 1) < ROWS), 1.0, 0.0
        ).astype(BF16).reshape(NBLK, BS, 2 * ROWS)
        widen(odd)

    fetches[0].wait()
    fetches[5].wait()
    pl.semaphore_wait(barrier, GROUP - odd + meets)

    def piece(n, p):
        return comp.at[n, span_of(p), :]

    def give_step(n):
        mine = piece(n, i)
        send(mine, mine, c_twin.at[n], c_core.at[n], (t, twin))
        send(mine, mine, c_send.at[n], c_far.at[n], (t, opposite))
        send(mine, mine, c_send.at[n], c_left.at[n], (t, above))
        send(mine, mine, c_send.at[n], c_right.at[n], (t, below))

    def pass_step(n):
        for p, sems in ((below, c_left), (above, c_right), (opposite, c_far)):
            part = piece(n, p)
            await_bytes(part, sems.at[n])
            send(part, part, c_twin.at[n], c_core.at[n], (t, twin))

    def hand_over(k):
        ref = piece(k, i)
        send(ref, ref, c_over.at[k], c_mine.at[k], (lead, i))

    def own_rows_out():
        for d in (4, 5, 3, 2, 6, 7, 1):
            j = (i + d) % GROUP
            send(
                columns_of.at[0, span_of(j), :], rows_out.at[:, own], swap_send, swap_recv, (t, j)
            )
        rows_out[:, own] = columns_of[0, own, :]

    last_step = STRETCH * (1 + odd)

    def step(n, carry):
        @pl.when(n + 1 < last_step)
        def _():
            pass_step(n + 1)

        @pl.when((odd == 1) & (n < 2))
        def _():
            give_step(n + 6)

        await_bytes(comp.at[n, pl.ds(0, 4 * ROWS), :], c_core.at[n])
        for part in range(GROUP):
            rows = slice(part * ROWS, (part + 1) * ROWS)
            products = []
            for r in range(part * GROUP, (part + 1) * GROUP):
                chosen = jnp.concatenate([state[pattern[s, r]] for s in range(S)], axis=0)
                products.append(dot(comp[n, r * BS : (r + 1) * BS, :], chosen))
            wide = damp_wide[n, rows, :]
            old = state[part * GROUP : (part + 1) * GROUP].reshape(ROWS, 2 * ROWS)
            value = old.astype(F32) * jnp.concatenate([wide, wide], axis=1)
            value = value + jnp.concatenate(products, axis=0)
            mixed[rows, :] = value
            mixed_b[rows, :] = value.astype(BF16)
        quarter = STATES // 4
        seen = sum(
            dot(pick[:, q * quarter : (q + 1) * quarter], mixed_b[q * quarter : (q + 1) * quarter, :])
            for q in range(4)
        )
        lane = iota((SENSORS, ROWS), 1)
        readings = jnp.where(lane == 0, obs_wide[n], 0.0)
        seen = jnp.concatenate([seen[:, :ROWS], seen[:, ROWS:] - readings], axis=1).astype(BF16)
        for q in range(4):
            rows = slice(q * quarter, (q + 1) * quarter)
            value = mixed[rows, :] - dot(gain[rows, :], seen)
            state[q * 16 : (q + 1) * 16] = value.astype(BF16).reshape(16, BS, 2 * ROWS)
            vector_f[rows, :] = value[:, ROWS:]

        return carry

    def rows_at(m):
        return span_of(m % PARTS, CHUNK)

    def give_vector(level):
        value = vec_row[0:1, :]
        high = value.astype(BF16).astype(F32)
        row = iota((16, STATES), 0)
        both = jnp.where(
            row == 0, jnp.broadcast_to(high, (16, STATES)),
            jnp.where(row == 1, jnp.broadcast_to(value - high, (16, STATES)), 0.0),
        )
        vec_send[...] = both.astype(BF16)
        send(vec_send, vec_in.at[level], vec_sends, vec_recv.at[level], (t + SPANS[level], i))

    def give_up(level, m):
        rows = rows_at(m)
        send(
            columns_of.at[level, rows, :], earlier.at[level, rows, :],
            up_send.at[m % PARTS], up_recv.at[level * PARTS + m % PARTS], (t + SPANS[level], i),
        )

    def give_part(m):
        level = m // PARTS
        rows = rows_at(m)
        src = columns_of.at[level, rows, :]
        dst = whole.at[level, rows, own]
        send(src, dst, m_send.at[m], m_far.at[m], (t, opposite))
        send(src, dst, m_send.at[m], m_left.at[m], (t, above))
        send(src, dst, m_send.at[m], m_right.at[m], (t, below))
        send(src, dst, m_twin.at[m], m_core.at[m], (t, twin))
        whole[level, rows, own] = columns_of[level, rows, :]

    def pass_part(m):
        for p, sems in ((below, m_left), (above, m_right), (opposite, m_far)):
            part = whole.at[m // PARTS, rows_at(m), span_of(p)]
            await_bytes(part, sems.at[m])
            send(part, part, m_twin.at[m], m_core.at[m], (t, twin))

    def give_row(j):
        block = columns_of.at[merges, span_of(j), :]

        @pl.when(j != i)
        def _():
            send(block, rows_out.at[:, own], swap_send, swap_recv, (t, j))

        @pl.when(j == i)
        def _():
            rows_out[:, own] = columns_of[merges, own, :]

    def merge(m, carry):
        level = m // PARTS
        r = m % PARTS
        rows = rows_at(m)

        @pl.when(r == 0)
        def _():
            pass_part(m)

        @pl.when((level == 0) & (r == 0) & (PACE < PARTS))
        def _():
            give_part(PACE)

        @pl.when(r + 1 < PARTS)
        def _():
            pass_part(m + 1)

        @pl.when((level == 0) & (r + 1 + PACE < PARTS))
        def _():
            give_part(m + 1 + PACE)

        @pl.when(r == 0)
        def _():
            for q in range(PARTS):
                await_bytes(
                    earlier.at[level, pl.ds(q * CHUNK, CHUNK), :], up_recv.at[level * PARTS + q]
                )

        await_bytes(whole.at[level, rows, pl.ds(0, 4 * ROWS)], m_core.at[m])
        columns_of[level + 1, rows, :] = dot(whole[level, rows, :], earlier[level]).astype(BF16)

        @pl.when(level + 1 < merges)
        def _():
            give_part(m + PARTS)

        @pl.when(level + 1 == merges)
        def _():
            for d in range(CHUNK // ROWS):
                give_row(r * (CHUNK // ROWS) + d)

        for at in (1, 2):
            @pl.when(producer[at] & (level == at - 1))
            def _():
                give_up(at, m)

        @pl.when(r == PARTS - 1)
        def _():
            await_bytes(vec_in.at[level], vec_recv.at[level])
            found = lax.dot_general(
                vec_in[level], whole[level], (((1,), (1,)), ((), ())),
                preferred_element_type=F32,
            )
            vec_row[0:1, :] = vec_row[0:1, :] + found[0:1, :] + found[1:2, :]

            for at in (1, 2):
                @pl.when(producer[at] & (level == at - 1))
                def _():
                    give_vector(at)

        return carry

    @pl.when(odd == 0)
    def _():
        send(small.at[0], small.at[0], small_send, small_recv, (lead, i))
        for k in range(STRETCH):
            give_step(k)
            hand_over(k)
        pass_step(0)

    @pl.when(odd == 1)
    def _():
        give_step(STRETCH)
        give_step(STRETCH + 1)
        await_bytes(small.at[0], small_recv)
        widen(0)
        for k in range(STRETCH):
            await_bytes(piece(k, i), c_mine.at[k])
            give_step(k)
        pass_step(0)

    lax.fori_loop(0, last_step, step, 0)
    columns_of[0] = state[:, :, 0:ROWS].reshape(STATES, ROWS)

    @pl.when(merges > 0)
    def _():
        def give(m, carry):
            give_part(m)
            return carry

        lax.fori_loop(0, PACE, give, 0)

    @pl.when(producer[0])
    def _():
        for m in range(PARTS):
            give_up(0, m)

    for part in range(GROUP):
        rows = slice(part * ROWS, (part + 1) * ROWS)
        vec_row[0:1, rows] = jnp.transpose(vector_f[rows, :])[0:1, :]

    @pl.when(producer[0])
    def _():
        give_vector(0)

    @pl.when(merges == 0)
    def _():
        own_rows_out()

    lax.fori_loop(0, count, merge, 0)
    vector_out[...] = vec_row[0:1, own]

    def drained(n, carry):
        await_bytes(comp.at[n, pl.ds(0, 3 * ROWS), :], c_send.at[n])
        await_bytes(comp.at[n, pl.ds(0, 4 * ROWS), :], c_twin.at[n])
        return carry

    lax.fori_loop(0, last_step, drained, 0)

    @pl.when(odd == 0)
    def _():
        for k in range(STRETCH):
            await_bytes(piece(k, i), c_over.at[k])
        await_bytes(small.at[0], small_send)

    def drained_part(m, carry):
        rows = rows_at(m)
        await_bytes(whole.at[m // PARTS, rows, pl.ds(0, 3 * ROWS)], m_send.at[m])
        await_bytes(whole.at[m // PARTS, rows, pl.ds(0, 4 * ROWS)], m_twin.at[m])
        return carry

    lax.fori_loop(0, count, drained_part, 0)

    @pl.when(producer[0] | producer[1] | producer[2])
    def _():
        for q in range(PARTS):
            await_bytes(earlier.at[0, pl.ds(q * CHUNK, CHUNK), :], up_send.at[q])
        await_bytes(vec_send, vec_sends)

    await_bytes(rows_out.at[:, pl.ds(0, 7 * ROWS)], swap_recv)
    result = pltpu.make_async_copy(rows_out, matrix_out.at[0], out_sem)
    result.start()
    await_bytes(rows_out.at[:, pl.ds(0, 7 * ROWS)], swap_send)
    result.wait()


def shards(observations, gain, damping, blocks, pattern, sensor_index):
    anywhere = pl.BlockSpec(memory_space=pl.ANY)
    dma = pltpu.SemaphoreType.DMA
    merges = len(SPANS)
    moves = PARTS * merges
    return pl.pallas_call(
        kernel,
        out_shape=(
            jax.ShapeDtypeStruct((1, ROWS, STATES), BF16),
            jax.ShapeDtypeStruct((1, ROWS), F32),
        ),
        in_specs=[anywhere] * 6,
        out_specs=(anywhere, pl.BlockSpec(memory_space=pltpu.VMEM)),
        scratch_shapes=[
            pltpu.SMEM((S, NBLK), jnp.int32),
            pltpu.VMEM((1, SENSORS), jnp.int32),
            pltpu.VMEM((STRETCH, SENSORS), BF16),
            pltpu.VMEM((STATES, SENSORS), BF16),
            pltpu.VMEM((STRETCH, STATES), F32),
            pltpu.VMEM((STEPS, STATES, SENSORS), BF16),
            pltpu.VMEM((2, 8, STATES), F32),
            pltpu.VMEM((STEPS, STATES, ROWS), F32),
            pltpu.VMEM((STEPS, SENSORS, ROWS), F32),
            pltpu.VMEM((SENSORS, STATES), BF16),
            pltpu.VMEM((NBLK, BS, 2 * ROWS), BF16),
            pltpu.VMEM((STATES, 2 * ROWS), F32),
            pltpu.VMEM((STATES, 2 * ROWS), BF16),
            pltpu.VMEM((STATES, ROWS), F32),
            pltpu.VMEM((merges + 1, STATES, ROWS), BF16),
            pltpu.VMEM((merges, STATES, STATES), BF16),
            pltpu.VMEM((merges, STATES, ROWS), BF16),
            pltpu.VMEM((merges, 16, STATES), BF16),
            pltpu.VMEM((8, STATES), F32),
            pltpu.VMEM((16, STATES), BF16),
            pltpu.VMEM((ROWS, STATES), BF16),
            dma((6,)), dma, dma,
            *[dma((STEPS,))] * 8,
            *[dma((moves,))] * 6,
            dma((PARTS,)), dma((moves,)), dma, dma((merges,)), dma, dma, dma,
        ],
        compiler_params=pltpu.CompilerParams(
            collective_id=0, has_side_effects=True, vmem_limit_bytes=VMEM_BYTES
        ),
    )(pattern.T, sensor_index.reshape(1, SENSORS), observations, gain, damping, blocks)


def solution(mesh):
    return jax.shard_map(
        shards,
        mesh=mesh,
        in_specs=(P("tm", None), P(), P("tm", None), P("tm", "row", None), P(), P()),
        out_specs=(P("tm", "row", None), P("tm", "row")),
        check_vma=False,
    )
```

time: 76.8 us -> 73.1 us (0.952)
  the two profiles are of different devices: /device:TPU:481 before, /device:TPU:511 now
where the time goes in v3:
time: 73.1 us; the launch traced here: 73 us
  Pallas kernels  70.1 us (96%)
  local copies, waits for them, and re-layouts  2.18 us (3%)
    pallas_call x1, Pallas kernels, shards(): pl.pallas_call(kernel, out_shape=(jax.ShapeDtypeStruct((1, ROWS, STATES),...  70.1 us
    unnamed x4, local copies, waits for them, and re-layouts  2.18 us

profile of v3, /device:TPU:511, one launch (start us, length us, event | category | flops | bytes accessed | tf_op | source)
XLA Modules:
  0.0 73.0 jit_solution(13205112904151995817)
XLA Ops:
  0.6 70.1 %shard_map.77 = (bf16[1,128,1024]{2,1,0:T(8,128)(2,1)}, f32[1,128]{1,0:T(1,128)}) custom-call(s32[8,64]{1,0:T(8,128)} %bitcast.2, s32[1,128]{1,0:T(1,128)} %bitcast.3, bf16[4,128]{1,0:T(4,128)(2,1)} %observations_in.1, bf16[1024,128]{1,0:T(8,128)(2,1)} %gain_in.1, f32[4,1024]{1,0:T(4,128)} %damping_in.1, bf16[4,128,128]{2,1,0:T(8,128)(2,1)} %blocks.1), custom_call_target="tpu_custom_call" | custom-call | tf_op jit(solution)/shard_map/pallas_call | solution.py:408
  70.8 0.0 copy-start
  70.8 1.7 %copy.10 = bf16[1,128,1024]{2,1,0:T(8,128)(2,1)} copy(bf16[1,128,1024]{2,1,0:T(8,128)(2,1)} %get-tuple-element.4) | data formatting | bytes 524288
  72.4 0.0 copy-done
  72.4 0.5 copy.11
Async XLA Ops:
  70.8 1.7 %copy-start = (f32[1,128]{1,0:T(1,128)S(1)}, f32[1,128]{1,0:T(1,128)}, u32[]{:S(2)}) copy-start(f32[1,128]{1,0:T(1,128)} %get-tuple-element.5) | copy-start | bytes 1540

commit v4 on v3

--- a/solution.py
+++ b/solution.py
@@ -43,7 +43,7 @@
     in_sems, small_send, small_recv,
     c_send, c_over, c_twin, c_mine, c_left, c_right, c_far, c_core,
     m_send, m_twin, m_left, m_right, m_far, m_core,
-    up_send, up_recv, vec_sends, vec_recv, swap_send, swap_recv, out_sem,
+    up_send, up_recv, vec_sends, vec_recv, swap_send, swap_recv,
 ):
     t = lax.axis_index("tm")
     i = lax.axis_index("row")
@@ -103,14 +103,6 @@
     for d in range(1, GROUP):
         greet((t, (i + d) % GROUP))
 
-    for fetch in fetches[1:3]:
-        fetch.wait()
-    small[odd] = jnp.zeros((8, STATES), F32)
-    small[odd, 0:STRETCH, :] = damping[...]
-    small[odd, STRETCH:8, 0:SENSORS] = observations[...].astype(F32)
-    for fetch in fetches[3:5]:
-        fetch.wait()
-
     def widen(b):
         columns = jnp.transpose(small[b])
         for k in range(STRETCH):
@@ -119,23 +111,7 @@
                 columns[:SENSORS, STRETCH + k : STRETCH + k + 1], (SENSORS, ROWS)
             )
 
-    if True:
-        eye = iota((SENSORS, SENSORS), 0) == iota((SENSORS, SENSORS), 1)
-        sensor_col = jnp.sum(
-            jnp.where(eye, jnp.broadcast_to(sensor[...].astype(F32), (SENSORS, SENSORS)), 0.0),
-            axis=1, keepdims=True,
-        )
-        pick[...] = jnp.where(
-            sensor_col == iota((SENSORS, STATES), 1).astype(F32), 1.0, 0.0
-        ).astype(BF16)
-        first = iota((STATES, 2 * ROWS), 0) == iota((STATES, 2 * ROWS), 1) + i * ROWS
-        state[...] = jnp.where(
-            first & (iota((STATES, 2 * ROWS), 1) < ROWS), 1.0, 0.0
-        ).astype(BF16).reshape(NBLK, BS, 2 * ROWS)
-        widen(odd)
-
     fetches[0].wait()
-    fetches[5].wait()
     pl.semaphore_wait(barrier, GROUP - odd + meets)
 
     def piece(n, p):
@@ -318,23 +294,50 @@
 
     @pl.when(odd == 0)
     def _():
-        send(small.at[0], small.at[0], small_send, small_recv, (lead, i))
         for k in range(STRETCH):
             give_step(k)
             hand_over(k)
-        pass_step(0)
 
     @pl.when(odd == 1)
     def _():
         give_step(STRETCH)
         give_step(STRETCH + 1)
-        await_bytes(small.at[0], small_recv)
-        widen(0)
+
+    for fetch in fetches[1:]:
+        fetch.wait()
+    small[odd] = jnp.zeros((8, STATES), F32)
+    small[odd, 0:STRETCH, :] = damping[...]
+    small[odd, STRETCH:8, 0:SENSORS] = observations[...].astype(F32)
+
+
+    @pl.when(odd == 0)
+    def _():
+        send(small.at[0], small.at[0], small_send, small_recv, (lead, i))
+
+    eye = iota((SENSORS, SENSORS), 0) == iota((SENSORS, SENSORS), 1)
+    sensor_col = jnp.sum(
+        jnp.where(eye, jnp.broadcast_to(sensor[...].astype(F32), (SENSORS, SENSORS)), 0.0),
+        axis=1, keepdims=True,
+    )
+    pick[...] = jnp.where(
+        sensor_col == iota((SENSORS, STATES), 1).astype(F32), 1.0, 0.0
+    ).astype(BF16)
+    first = iota((STATES, 2 * ROWS), 0) == iota((STATES, 2 * ROWS), 1) + i * ROWS
+    state[...] = jnp.where(
+        first & (iota((STATES, 2 * ROWS), 1) < ROWS), 1.0, 0.0
+    ).astype(BF16).reshape(NBLK, BS, 2 * ROWS)
+    widen(odd)
+
+
+    @pl.when(odd == 1)
+    def _():
         for k in range(STRETCH):
             await_bytes(piece(k, i), c_mine.at[k])
             give_step(k)
-        pass_step(0)
-
+        await_bytes(small.at[0], small_recv)
+        widen(0)
+
+    pass_step(0)
     lax.fori_loop(0, last_step, step, 0)
     columns_of[0] = state[:, :, 0:ROWS].reshape(STATES, ROWS)
 
@@ -394,10 +397,8 @@
         await_bytes(vec_send, vec_sends)
 
     await_bytes(rows_out.at[:, pl.ds(0, 7 * ROWS)], swap_recv)
-    result = pltpu.make_async_copy(rows_out, matrix_out.at[0], out_sem)
-    result.start()
+    matrix_out[0] = rows_out[...]
     await_bytes(rows_out.at[:, pl.ds(0, 7 * ROWS)], swap_send)
-    result.wait()
 
 
 def shards(observations, gain, damping, blocks, pattern, sensor_index):
@@ -408,11 +409,11 @@
     return pl.pallas_call(
         kernel,
         out_shape=(
-            jax.ShapeDtypeStruct((1, ROWS, STATES), BF16),
-            jax.ShapeDtypeStruct((1, ROWS), F32),
+            pltpu.VMEM((1, ROWS, STATES), BF16),
+            pltpu.VMEM((1, ROWS), F32),
         ),
         in_specs=[anywhere] * 6,
-        out_specs=(anywhere, pl.BlockSpec(memory_space=pltpu.VMEM)),
+        out_specs=(pl.BlockSpec(memory_space=pltpu.VMEM),) * 2,
         scratch_shapes=[
             pltpu.SMEM((S, NBLK), jnp.int32),
             pltpu.VMEM((1, SENSORS), jnp.int32),
@@ -438,7 +439,7 @@
             dma((6,)), dma, dma,
             *[dma((STEPS,))] * 8,
             *[dma((moves,))] * 6,
-            dma((PARTS,)), dma((moves,)), dma, dma((merges,)), dma, dma, dma,
+            dma((PARTS,)), dma((moves,)), dma, dma((merges,)), dma, dma,
         ],
         compiler_params=pltpu.CompilerParams(
             collective_id=0, has_side_effects=True, vmem_limit_bytes=VMEM_BYTES

time: 73.1 us -> 70.9 us (0.970)
  the two profiles are of different devices: /device:TPU:511 before, /device:TPU:481 now
where the time goes in v4:
time: 70.9 us; the launch traced here: 70 us
  Pallas kernels  68.1 us (96%)
  local copies, waits for them, and re-layouts  1.22 us (2%)
    pallas_call x1, Pallas kernels, shards(): pl.pallas_call(kernel, out_shape=(pltpu.VMEM((1, ROWS, STATES), BF16), pl...  68.1 us

profile of v4, /device:TPU:481, one launch (start us, length us, event | category | flops | bytes accessed | tf_op | source)
XLA Modules:
  0.0 70.0 jit_solution(6067437205292103190)
XLA Ops:
  0.6 68.1 %shard_map.77 = (bf16[1,128,1024]{2,1,0:T(8,128)(2,1)S(1)}, f32[1,128]{1,0:T(1,128)S(1)}) custom-call(s32[8,64]{1,0:T(8,128)} %bitcast.2, s32[1,128]{1,0:T(1,128)} %bitcast.3, bf16[4,128]{1,0:T(4,128)(2,1)} %observations_in.1, bf16[1024,128]{1,0:T(8,128)(2,1)} %gain_in.1, f32[4,1024]{1,0:T(4,128)} %damping_in.1, bf16[4,128,128]{2,1,0:T(8,128)(2,1)} %blocks.1), custom_call_target="tpu_custom_call" | custom-call | tf_op jit(solution)/shard_map/pallas_call | solution.py:409
  68.7 0.7 %copy.10 = bf16[1,128,1024]{2,1,0:T(8,128)(2,1)} copy(bf16[1,128,1024]{2,1,0:T(8,128)(2,1)S(1)} %get-tuple-element.2) | data formatting | bytes 524288
  69.5 0.5 copy.11

commit v5 on v4

--- a/solution.py
+++ b/solution.py
@@ -149,9 +149,9 @@
         def _():
             pass_step(n + 1)
 
-        @pl.when((odd == 1) & (n < 2))
-        def _():
-            give_step(n + 6)
+        @pl.when((odd == 1) & (n < 3))
+        def _():
+            give_step(n + 5)
 
         await_bytes(comp.at[n, pl.ds(0, 4 * ROWS), :], c_core.at[n])
         for part in range(GROUP):
@@ -208,9 +208,9 @@
         rows = rows_at(m)
         src = columns_of.at[level, rows, :]
         dst = whole.at[level, rows, own]
-        send(src, dst, m_send.at[m], m_far.at[m], (t, opposite))
         send(src, dst, m_send.at[m], m_left.at[m], (t, above))
         send(src, dst, m_send.at[m], m_right.at[m], (t, below))
+        send(src, dst, m_send.at[m], m_far.at[m], (t, opposite))
         send(src, dst, m_twin.at[m], m_core.at[m], (t, twin))
         whole[level, rows, own] = columns_of[level, rows, :]
 
@@ -240,15 +240,15 @@
         def _():
             pass_part(m)
 
-        @pl.when((level == 0) & (r == 0) & (PACE < PARTS))
-        def _():
-            give_part(PACE)
+        @pl.when((r == 0) & (PACE < PARTS))
+        def _():
+            give_part(m + PACE)
 
         @pl.when(r + 1 < PARTS)
         def _():
             pass_part(m + 1)
 
-        @pl.when((level == 0) & (r + 1 + PACE < PARTS))
+        @pl.when(r + 1 + PACE < PARTS)
         def _():
             give_part(m + 1 + PACE)
 
@@ -262,7 +262,7 @@
         await_bytes(whole.at[level, rows, pl.ds(0, 4 * ROWS)], m_core.at[m])
         columns_of[level + 1, rows, :] = dot(whole[level, rows, :], earlier[level]).astype(BF16)
 
-        @pl.when(level + 1 < merges)
+        @pl.when((level + 1 < merges) & (r < PACE))
         def _():
             give_part(m + PARTS)
 
@@ -292,27 +292,23 @@
 
         return carry
 
+    def begin_even(k):
+        hand_over(k)
+        give_step(k)
+
     @pl.when(odd == 0)
     def _():
-        for k in range(STRETCH):
-            give_step(k)
-            hand_over(k)
+        begin_even(0)
 
     @pl.when(odd == 1)
     def _():
         give_step(STRETCH)
-        give_step(STRETCH + 1)
 
     for fetch in fetches[1:]:
         fetch.wait()
     small[odd] = jnp.zeros((8, STATES), F32)
     small[odd, 0:STRETCH, :] = damping[...]
     small[odd, STRETCH:8, 0:SENSORS] = observations[...].astype(F32)
-
-
-    @pl.when(odd == 0)
-    def _():
-        send(small.at[0], small.at[0], small_send, small_recv, (lead, i))
 
     eye = iota((SENSORS, SENSORS), 0) == iota((SENSORS, SENSORS), 1)
     sensor_col = jnp.sum(
@@ -322,12 +318,26 @@
     pick[...] = jnp.where(
         sensor_col == iota((SENSORS, STATES), 1).astype(F32), 1.0, 0.0
     ).astype(BF16)
+
+    @pl.when(odd == 0)
+    def _():
+        begin_even(1)
+        send(small.at[0], small.at[0], small_send, small_recv, (lead, i))
+
     first = iota((STATES, 2 * ROWS), 0) == iota((STATES, 2 * ROWS), 1) + i * ROWS
     state[...] = jnp.where(
         first & (iota((STATES, 2 * ROWS), 1) < ROWS), 1.0, 0.0
     ).astype(BF16).reshape(NBLK, BS, 2 * ROWS)
+
+    @pl.when(odd == 0)
+    def _():
+        begin_even(2)
+
     widen(odd)
 
+    @pl.when(odd == 0)
+    def _():
+        begin_even(3)
 
     @pl.when(odd == 1)
     def _():

time: 70.9 us -> 69 us (0.973)
  Pallas kernels: 68.1 us -> 66.6 us
    pallas_call x1, Pallas kernels: 68.1 us -> 66.6 us  [shards(): pl.pallas_call(kernel, out_shape=(pltpu.VMEM((1, ROWS, STATES), BF16), pl...]
where the time goes in v5:
time: 69 us; the launch traced here: 68.5 us
  Pallas kernels  66.6 us (97%)
  local copies, waits for them, and re-layouts  1.22 us (2%)
    pallas_call x1, Pallas kernels, shards(): pl.pallas_call(kernel, out_shape=(pltpu.VMEM((1, ROWS, STATES), BF16), pl...  66.6 us

profile of v5, /device:TPU:481, one launch (start us, length us, event | category | flops | bytes accessed | tf_op | source)
XLA Modules:
  0.0 68.5 jit_solution(1589323769656624864)
XLA Ops:
  0.6 66.6 %shard_map.77 = (bf16[1,128,1024]{2,1,0:T(8,128)(2,1)S(1)}, f32[1,128]{1,0:T(1,128)S(1)}) custom-call(s32[8,64]{1,0:T(8,128)} %bitcast.2, s32[1,128]{1,0:T(1,128)} %bitcast.3, bf16[4,128]{1,0:T(4,128)(2,1)} %observations_in.1, bf16[1024,128]{1,0:T(8,128)(2,1)} %gain_in.1, f32[4,1024]{1,0:T(4,128)} %damping_in.1, bf16[4,128,128]{2,1,0:T(8,128)(2,1)} %blocks.1), custom_call_target="tpu_custom_call" | custom-call | tf_op jit(solution)/shard_map/pallas_call | solution.py:419
  67.3 0.7 %copy.10 = bf16[1,128,1024]{2,1,0:T(8,128)(2,1)} copy(bf16[1,128,1024]{2,1,0:T(8,128)(2,1)S(1)} %get-tuple-element.2) | data formatting | bytes 524288
  68.0 0.5 copy.11

commit v6 on v5

--- a/solution.py
+++ b/solution.py
@@ -208,10 +208,10 @@
         rows = rows_at(m)
         src = columns_of.at[level, rows, :]
         dst = whole.at[level, rows, own]
+        send(src, dst, m_twin.at[m], m_core.at[m], (t, twin))
         send(src, dst, m_send.at[m], m_left.at[m], (t, above))
         send(src, dst, m_send.at[m], m_right.at[m], (t, below))
         send(src, dst, m_send.at[m], m_far.at[m], (t, opposite))
-        send(src, dst, m_twin.at[m], m_core.at[m], (t, twin))
         whole[level, rows, own] = columns_of[level, rows, :]
 
     def pass_part(m):

time: 69 us -> 69 us (level)
  no operation moved by 1% of the time
where the time goes in v6:
time: 69 us; the launch traced here: 68.5 us
  Pallas kernels  66.6 us (97%)
  local copies, waits for them, and re-layouts  1.22 us (2%)
    pallas_call x1, Pallas kernels, shards(): pl.pallas_call(kernel, out_shape=(pltpu.VMEM((1, ROWS, STATES), BF16), pl...  66.6 us

profile of v6, /device:TPU:481, one launch (start us, length us, event | category | flops | bytes accessed | tf_op | source)
XLA Modules:
  0.0 68.5 jit_solution(6921635180761319584)
XLA Ops:
  0.6 66.6 %shard_map.77 = (bf16[1,128,1024]{2,1,0:T(8,128)(2,1)S(1)}, f32[1,128]{1,0:T(1,128)S(1)}) custom-call(s32[8,64]{1,0:T(8,128)} %bitcast.2, s32[1,128]{1,0:T(1,128)} %bitcast.3, bf16[4,128]{1,0:T(4,128)(2,1)} %observations_in.1, bf16[1024,128]{1,0:T(8,128)(2,1)} %gain_in.1, f32[4,1024]{1,0:T(4,128)} %damping_in.1, bf16[4,128,128]{2,1,0:T(8,128)(2,1)} %blocks.1), custom_call_target="tpu_custom_call" | custom-call | tf_op jit(solution)/shard_map/pallas_call | solution.py:419
  67.3 0.7 %copy.10 = bf16[1,128,1024]{2,1,0:T(8,128)(2,1)} copy(bf16[1,128,1024]{2,1,0:T(8,128)(2,1)S(1)} %get-tuple-element.2) | data formatting | bytes 524288
  68.0 0.5 copy.11
